TPU v7x, 32 devices: a whole 2x2x4 slice. The times are simulated.
32 devices in a mesh: groups: 2 (over y), tp: 4 (over z), rows: 4 (over x, core).
Axes of the slice: x: 2, y: 2, z: 4, core: 2. Of those that a mesh axis runs over, the one named last changes fastest.
Arguments:
- hidden: bfloat16 [512, 28672], P(('groups', 'tp'), 'rows'), parts along dimension 0, may hold values from -6 to 6
- down_weight: bfloat16 [28672, 8192], P('rows', 'tp'), may hold values from -0.03125 to 0.03125
- adapter_first_factors: bfloat16 [8, 28672, 64], P('tp', 'rows'), may hold values from -0.03125 to 0.03125
- adapter_second_factors: bfloat16 [8, 64, 8192], P('rows', None, 'tp'), may hold values from -0.75 to 0.75
- segment_lengths: int32 [8, 4], P('groups'), parts along dimension 0, may hold values from 1 to 32, 64 in all within a row
- segment_adapter: int32 [8, 4], P('groups'), parts along dimension 0, may hold values from 0 to 7
- adapter_slot: int32 [8], replicated, may hold values from 0 to 7, each once
Outputs:
- mixed: bfloat16 [512, 8192], P(('groups', 'rows'), 'tp'), parts along dimension 0
There are 2 independent parts, one for each index of `groups`. A program takes and returns all parts, laid end to end along the dimension named above; an argument that names none is the same for every part. Nothing has to cross between parts.
Inputs may be any that keep to these rules, and one draw needn't show every extreme that they name: Each row of segment_lengths sums to 64 and its largest entry is 32. `adapter_slot`: names every slot once.
All inputs are finite; a program needn't handle non-finite values.
Results may differ from a plain program's by a relative error of at most 0.0065.
Values may be sent and summed in bfloat16 or wider, within the bound.
A program may use at most 128 MiB of HBM per device.

v0:
```python
import jax
import jax.numpy as jnp
from jax import lax
from jax.sharding import PartitionSpec as P


def slot_table(segment_lengths, segment_adapter, adapter_slot, rows_each):
    ends = jnp.cumsum(segment_lengths, axis=1)
    position = lax.broadcasted_iota(jnp.int32, (1, rows_each, 1), 1)
    segment = jnp.sum((position >= ends[:, None, :]).astype(jnp.int32), axis=2)
    seg_count = segment_lengths.shape[1]
    picks = segment[:, :, None] == lax.broadcasted_iota(jnp.int32, (1, 1, seg_count), 2)
    adapter = jnp.sum(picks.astype(jnp.int32) * segment_adapter[:, None, :], axis=2).reshape(-1)
    adapter_count = adapter_slot.shape[0]
    hits = adapter[:, None] == lax.broadcasted_iota(jnp.int32, (1, adapter_count), 1)
    return jnp.sum(hits.astype(jnp.int32) * adapter_slot[None, :], axis=1)


def reduce_shrink(partial_low):
    return lax.psum(partial_low, ("tp", "rows"))


def local(
    hidden,
    down_weight,
    adapter_first_factors,
    adapter_second_factors,
    segment_lengths,
    segment_adapter,
    adapter_slot,
):
    rows_each = hidden.shape[0]
    row_slot = slot_table(segment_lengths, segment_adapter, adapter_slot, rows_each)
    total_rows = row_slot.shape[0]
    first_factor_count = adapter_first_factors.shape[0]
    second_factor_count = adapter_second_factors.shape[0]
    rank_columns = adapter_first_factors.shape[2]
    a_first = lax.axis_index("tp") * first_factor_count
    b_first = lax.axis_index("rows") * second_factor_count
    a_pick = (
        row_slot[:, None] == a_first + lax.broadcasted_iota(jnp.int32, (1, first_factor_count), 1)
    ).astype(jnp.float32)
    b_pick = (
        row_slot[:, None] == b_first + lax.broadcasted_iota(jnp.int32, (1, second_factor_count), 1)
    ).astype(jnp.float32)
    segment_piece = lax.all_gather(hidden, "tp", axis=0, tiled=True)
    part = jnp.dot(segment_piece, down_weight, preferred_element_type=jnp.float32)
    adapter_product = jnp.einsum(
        "dm,jmh->djh", segment_piece, adapter_first_factors, preferred_element_type=jnp.float32
    )
    low_acc = jnp.sum(adapter_product * a_pick[:, :, None], axis=1)
    low_full = reduce_shrink(low_acc)
    spread = (b_pick[:, :, None] * low_full[:, None, :]).reshape(
        total_rows, second_factor_count * rank_columns
    )
    upper = spread.astype(jnp.bfloat16)
    lower = (spread - upper.astype(jnp.float32)).astype(jnp.bfloat16)
    factor_pairs = adapter_second_factors.reshape(
        second_factor_count * rank_columns, adapter_second_factors.shape[2]
    )
    low_rank = jnp.dot(upper, factor_pairs, preferred_element_type=jnp.float32) + jnp.dot(
        lower, factor_pairs, preferred_element_type=jnp.float32
    )
    prompt_block = lax.psum_scatter(part + low_rank, "rows", scatter_dimension=0, tiled=True)
    return prompt_block.astype(jnp.bfloat16)


def solution(mesh):
    placed = (
        P(("groups", "tp"), "rows"),
        P("rows", "tp"),
        P("tp", "rows", None),
        P("rows", None, "tp"),
        P("groups", None),
        P("groups", None),
        P(),
    )
    return jax.shard_map(
        local, mesh=mesh, in_specs=placed, out_specs=P(("groups", "rows"), "tp"), check_vma=False
    )
```

profile of v0, /device:TPU:0, one launch (start us, length us, event | category | flops | bytes accessed | tf_op | source)
XLA Modules:
  0.0 231.0 jit_solution(13997388935081166049)
XLA Ops:
  6.5 0.0 copy-start
  6.5 0.0 all-gather.2.cloned.1.call-start
  6.5 0.7 all-gather.2.cloned.1.call-update
  7.3 0.0 all-reduce.2.cloned.1.call-start
  7.3 0.9 reduce_window_sum.11
  8.2 0.1 convert_reduce_fusion
  8.3 0.8 select_reduce_fusion.1
  9.0 0.1 eq.63
  9.1 0.7 select_reduce_fusion
  9.8 0.1 compare_convert_fusion.1
  9.9 73.8 %all-gather.2.cloned.1.call-done = bf16[256,7168]{1,0:T(8,128)(2,1)} async-done(((bf16[64,7168]{1,0:T(8,128)(2,1)}), bf16[256,7168]{1,0:T(8,128)(2,1)}) %all-gather.2.cloned.1.call-update) | async-done | bytes 3670032 | tf_op jit(solution)/shard_map/all_gather | solution.py:46
  83.8 0.0 copy-done
  83.8 0.0 copy-start.2
  83.8 3.4 %fusion.7 = f32[256,128]{0,1:S(1)} fusion(bf16[256,7168]{1,0:T(8,128)(2,1)} %all-gather.2.cloned.1.call-done, bf16[7168,128]{0,1:T(8,128)(2,1)S(1)} %bitcast.16), kind=kOutput, calls=%fused_computation.22 | convolution fusion | flops 469762048 | bytes 5636096
  87.2 0.6 multiply_reduce_fusion
  87.9 0.0 all-reduce.2.cloned.1.call-update
  87.9 0.0 reduce-scatter.2.cloned.1.call-start
  87.9 83.2 %all-reduce.2.cloned.1.call-done = f32[256,64]{0,1:T(8,128)} async-done(((f32[256,64]{0,1:T(8,128)}), f32[256,64]{0,1:T(8,128)}) %all-reduce.2.cloned.1.call-update) | async-done | bytes 65552 | tf_op jit(solution)/shard_map/psum | solution.py:20
  171.1 0.0 copy-start.3
  171.1 0.0 copy-done.2
  171.1 1.4 convolution_bitcast_fusion
  172.5 0.0 copy-done.3
  172.5 0.0 copy-start.1
  172.5 0.5 fusion
  173.0 1.6 copy-done.1
  174.5 14.9 %convolution_add_fusion = f32[256,2048]{1,0:T(8,128)} fusion(f32[256,2048]{1,0:T(8,128)S(1)} %fusion, bf16[256,7168]{1,0:T(8,128)(2,1)S(1)} %copy-done.1, bf16[7168,2048]{1,0:T(8,128)(2,1)} %param.8), kind=kOutput, calls=%fused_computation.2 | convolution fusion | flops 7516717056 | bytes 37224448 | tf_op jit(solution)/shard_map/dot_general | solution.py:47
  189.5 0.0 reduce-scatter.2.cloned.1.call-update
  189.5 33.2 %reduce-scatter.2.cloned.1.call-done = f32[64,2048]{1,0:T(8,128)} async-done(((f32[256,2048]{1,0:T(8,128)}), f32[64,2048]{1,0:T(8,128)}) %reduce-scatter.2.cloned.1.call-update) | async-done | bytes 524304 | tf_op jit(solution)/shard_map/reduce_scatter | solution.py:64
  222.7 1.8 convert_element_type.41
  (1 shorter events, 0.0 us)
Async XLA Ops:
  6.5 77.2 %copy-start = (bf16[2,7168,64]{1,2,0:T(8,128)(2,1)S(1)}, bf16[2,7168,64]{1,2,0:T(8,128)(2,1)}, u32[]{:S(2)}) copy-start(bf16[2,7168,64]{1,2,0:T(8,128)(2,1)} %param.9) | copy-start | bytes 5505028
  6.5 77.2 %all-gather.2.cloned.1.call-start = ((), (), s32[]{:S(2)}) async-start(), calls=%async_computation.1 | async-start | bytes 4587520 | tf_op jit(solution)/shard_map/all_gather | solution.py:46
  7.3 163.8 %all-reduce.2.cloned.1.call-start = ((), (), s32[]{:S(2)}) async-start(), calls=%async_computation.2 | async-start | bytes 131072 | tf_op jit(solution)/shard_map/psum | solution.py:20
  83.8 87.3 %copy-start.2 = (bf16[2,64,2048]{2,1,0:T(8,128)(2,1)S(1)}, bf16[2,64,2048]{2,1,0:T(8,128)(2,1)}, u32[]{:S(2)}) copy-start(bf16[2,64,2048]{2,1,0:T(8,128)(2,1)} %param.10) | copy-start | bytes 1572868
  87.9 134.8 %reduce-scatter.2.cloned.1.call-start = ((), (), s32[]{:S(2)}) async-start(), calls=%async_computation.3 | async-start | bytes 2621440 | tf_op jit(solution)/shard_map/reduce_scatter | solution.py:64
  171.1 1.4 copy-start.3
  172.5 2.0 copy-start.1
Sparse Core Ops, SparseCore 0:
  8.9 74.7 all-gather.1
  88.0 83.0 all-reduce.1
  189.6 33.0 reduce-scatter.1
where the time goes:
time: 231 us
  waiting for transfers between devices  191 us (83%)
  matrix products  20.2 us (9%)
  between operations  13.2 us (6%)
  other arithmetic  4.94 us (2%)
    psum x1, waiting for transfers between devices, reduce_shrink(): return lax.psum(partial_low, ('tp', 'rows'))  83.2 us
    all_gather x1, waiting for transfers between devices, local(): segment_piece = lax.all_gather(hidden, 'tp', axis=0, tiled=True)  73.8 us
    reduce_scatter x1, waiting for transfers between devices, local(): lax.psum_scatter(part + low_rank, 'rows', scatter_dimension=0, tiled=True)  33.2 us
    dot_general x1, matrix products, local(): jnp.dot(segment_piece, down_weight, preferred_element_type=jnp.float32)  14.9 us
  transfers between devices with their start and end apart: 3, of which 3 were waited for; matrix products, arithmetic and copies ran while one was open for 1% of the time, Pallas kernels for 0%

commit v1 on v0

--- a/solution.py
+++ b/solution.py
@@ -1,6 +1,10 @@
+import functools
+
 import jax
 import jax.numpy as jnp
 from jax import lax
+from jax.experimental import pallas as pl
+from jax.experimental.pallas import tpu as pltpu
 from jax.sharding import PartitionSpec as P
 
 
@@ -65,6 +69,308 @@
     return prompt_block.astype(jnp.bfloat16)
 
 
+CHUNKS = 4
+TILE = 512
+MESH = pl.DeviceIdType.MESH
+
+
+def fused_kernel(
+    hid, w, a, b, seg_len, seg_ad, slot_of, out,
+    gath, wv, av, bv, acc, sh, stage, rbuf, shsel, shbuf, zsrc, zbuf,
+    own_sem, w_sem, a_sem, bown_sem, b_send, b_recv,
+    right_send, right_recv, left_send, left_recv,
+    base_send, base_recv, sh_send, sh_recv, z_send, z_recv,
+):
+    t, r = lax.axis_index("tp"), lax.axis_index("rows")
+    tp, chunks, rows_each, kc = gath.shape
+    nrows = rbuf.shape[0]
+    slots_each = av.shape[1]
+    rank = av.shape[3]
+    width = wv.shape[2]
+    tiles = width // TILE
+    up, down = lax.rem(t + 1, tp), lax.rem(t + tp - 1, tp)
+
+    def own_copy(c):
+        return pltpu.make_async_copy(
+            hid.at[:, pl.ds(pl.multiple_of(c * kc, kc), kc)], gath.at[t, c], own_sem.at[c]
+        )
+
+    def w_copy(c):
+        return pltpu.make_async_copy(
+            w.at[pl.ds(pl.multiple_of(c * kc, kc), kc), :], wv.at[c], w_sem.at[c]
+        )
+
+    def a_copy(c):
+        return pltpu.make_async_copy(
+            a.at[:, pl.ds(pl.multiple_of(c * kc, kc), kc), :], av.at[c], a_sem.at[c]
+        )
+
+    def b_own():
+        return pltpu.make_async_copy(b, bv.at[r], bown_sem)
+
+    def b_copy(d):
+        return pltpu.make_async_remote_copy(
+            src_ref=b, dst_ref=bv.at[r], send_sem=b_send.at[d - 1], recv_sem=b_recv.at[d - 1],
+            device_id={"rows": lax.rem(r + d, nrows)}, device_id_type=MESH,
+        )
+
+    def right(s, shard, c):
+        return pltpu.make_async_remote_copy(
+            src_ref=gath.at[shard, c], dst_ref=gath.at[shard, c],
+            send_sem=right_send.at[s, c], recv_sem=right_recv.at[s, c],
+            device_id={"tp": up}, device_id_type=MESH,
+        )
+
+    def left(s, shard, c):
+        return pltpu.make_async_remote_copy(
+            src_ref=gath.at[shard, c], dst_ref=gath.at[shard, c],
+            send_sem=left_send.at[s, c], recv_sem=left_recv.at[s, c],
+            device_id={"tp": down}, device_id_type=MESH,
+        )
+
+    def base_copy(j, slot, sem):
+        return pltpu.make_async_remote_copy(
+            src_ref=stage.at[j], dst_ref=rbuf.at[slot],
+            send_sem=base_send.at[j], recv_sem=base_recv.at[sem],
+            device_id={"rows": j}, device_id_type=MESH,
+        )
+
+    def sh_copy(j, slot, sem):
+        return pltpu.make_async_remote_copy(
+            src_ref=shsel.at[j], dst_ref=shbuf.at[slot],
+            send_sem=sh_send.at[j], recv_sem=sh_recv.at[sem],
+            device_id={"rows": j}, device_id_type=MESH,
+        )
+
+    def z_copy(d, slot):
+        return pltpu.make_async_remote_copy(
+            src_ref=zsrc, dst_ref=zbuf.at[slot],
+            send_sem=z_send.at[d - 1], recv_sem=z_recv.at[d - 1],
+            device_id={"tp": lax.rem(t + d, tp)}, device_id_type=MESH,
+        )
+
+    for c in range(chunks):
+        own_copy(c).start()
+    for c in range(chunks):
+        w_copy(c).start()
+        a_copy(c).start()
+    b_own().start()
+
+    barrier = pltpu.get_barrier_semaphore()
+    for d in range(1, tp):
+        pl.semaphore_signal(
+            barrier, inc=1, device_id={"tp": lax.rem(t + d, tp)}, device_id_type=MESH
+        )
+    for d in range(1, nrows):
+        pl.semaphore_signal(
+            barrier, inc=1, device_id={"rows": lax.rem(r + d, nrows)}, device_id_type=MESH
+        )
+    acc[...] = jnp.zeros_like(acc)
+    sh[...] = jnp.zeros_like(sh)
+    pl.semaphore_wait(barrier, tp - 1 + nrows - 1)
+
+    for c in range(chunks):
+        own_copy(c).wait()
+
+        @pl.when(t < tp - 1)
+        def _():
+            right(0, t, c).start()
+
+        @pl.when(t > 0)
+        def _():
+            left(0, t, c).start()
+
+    for d in range(1, nrows):
+        b_copy(d).start()
+
+    def slots_in(j):
+        position = lax.broadcasted_iota(jnp.int32, (rows_each, rank), 0)
+        slot = jnp.zeros((rows_each, rank), jnp.int32)
+        end = jnp.int32(0)
+        for k in range(seg_len.shape[1]):
+            slot = jnp.where(position >= end, slot_of[seg_ad[j, k]], slot)
+            end = end + seg_len[j, k]
+        return slot
+
+    def compute(shard, c):
+        for q in range(slots_each):
+            sh[shard, q] += jnp.dot(
+                gath[shard, c], av[c, q], preferred_element_type=jnp.float32
+            )
+
+        def tile_step(n, carry):
+            cols = pl.ds(pl.multiple_of(n * TILE, TILE), TILE)
+            acc[shard, :, cols] += jnp.dot(
+                gath[shard, c], wv[c, :, cols], preferred_element_type=jnp.float32
+            )
+            return carry
+
+        lax.fori_loop(0, tiles, tile_step, 0)
+
+    def finish(j):
+        slot = slots_in(j)
+        picked = jnp.zeros((rows_each, rank), jnp.float32)
+        for q in range(slots_each):
+            picked += jnp.where(slot == t * slots_each + q, sh[j, q], 0.0)
+        shsel[j] = picked
+
+        @pl.when(j != r)
+        def _():
+            sh_copy(j, r, r).start()
+            stage[j] = acc[j].astype(jnp.bfloat16)
+            base_copy(j, r, r).start()
+
+    def own_step(c, carry):
+        w_copy(c).wait()
+        a_copy(c).wait()
+        compute(t, c)
+        return carry
+
+    lax.fori_loop(0, chunks, own_step, 0)
+    finish(t)
+
+    def ring_step(i, carry):
+        s, c = i // chunks, i % chunks
+        low, high = t - 1 - s, t + 1 + s
+
+        @pl.when(low >= 0)
+        def _():
+            right(s, low, c).wait_recv()
+
+            @pl.when(t < tp - 1)
+            def _():
+                right(s + 1, low, c).start()
+
+            compute(low, c)
+
+            @pl.when(c == chunks - 1)
+            def _():
+                finish(low)
+
+        @pl.when(high <= tp - 1)
+        def _():
+            left(s, high, c).wait_recv()
+
+            @pl.when(t > 0)
+            def _():
+                left(s + 1, high, c).start()
+
+            compute(high, c)
+
+            @pl.when(c == chunks - 1)
+            def _():
+                finish(high)
+
+        return carry
+
+    lax.fori_loop(0, (tp - 1) * chunks, ring_step, 0)
+
+    total = shsel[r]
+    for d in range(1, nrows):
+        other = lax.rem(r + d, nrows)
+        sh_copy(other, other, other).wait_recv()
+        total = total + shbuf[other]
+    zsrc[...] = total
+    for d in range(1, tp):
+        z_copy(d, t).start()
+    b_own().wait()
+    for d in range(1, nrows):
+        b_copy(d).wait_recv()
+    slot = slots_in(r)
+    for d in range(1, tp):
+        source = lax.rem(t + tp - d, tp)
+        z_copy(d, source).wait_recv()
+        total = total + zbuf[source]
+    spread = jnp.concatenate(
+        [jnp.where(slot == q, total, 0.0) for q in range(slot_of.shape[0])], axis=1
+    )
+    upper = spread.astype(jnp.bfloat16)
+    lower = (spread - upper.astype(jnp.float32)).astype(jnp.bfloat16)
+    pair = jnp.concatenate([upper, lower], axis=0)
+    for d in range(1, nrows):
+        other = lax.rem(r + d, nrows)
+        base_copy(other, other, other).wait_recv()
+    depth = bv.shape[0] * bv.shape[1]
+    for n in range(tiles):
+        cols = slice(n * TILE, (n + 1) * TILE)
+        both = jnp.dot(
+            pair, bv[:, :, cols].reshape(depth, TILE), preferred_element_type=jnp.float32
+        )
+        value = both[:rows_each] + both[rows_each:] + acc[r, :, cols]
+        for d in range(1, nrows):
+            other = lax.rem(r + d, nrows)
+            value += rbuf[other, :, cols].astype(jnp.float32)
+        out[:, cols] = value.astype(out.dtype)
+
+    def drain(i, carry):
+        s, c = i // chunks, i % chunks
+
+        @pl.when((t < tp - 1) & (t - s >= 0))
+        def _():
+            right(s, t - s, c).wait_send()
+
+        @pl.when((t > 0) & (t + s <= tp - 1))
+        def _():
+            left(s, t + s, c).wait_send()
+
+        return carry
+
+    lax.fori_loop(0, (tp - 1) * chunks, drain, 0)
+    for d in range(1, nrows):
+        other = lax.rem(r + d, nrows)
+        b_copy(d).wait_send()
+        sh_copy(other, r, r).wait_send()
+        base_copy(other, r, r).wait_send()
+    for d in range(1, tp):
+        z_copy(d, t).wait_send()
+
+
+def fused(tp, nrows, hidden, down_weight, first, second, seg_len, seg_ad, slot_of):
+    rows_each, depth = hidden.shape
+    width = down_weight.shape[1]
+    kc = depth // CHUNKS
+    slots_each, _, rank = first.shape
+    owned = second.shape[0] * second.shape[1]
+    second = second.reshape(owned, width)
+    dma = pltpu.SemaphoreType.DMA
+    anywhere = pl.BlockSpec(memory_space=pl.ANY)
+    scalars = pl.BlockSpec(memory_space=pltpu.SMEM)
+    return pl.pallas_call(
+        fused_kernel,
+        out_shape=jax.ShapeDtypeStruct((rows_each, width), jnp.bfloat16),
+        in_specs=[anywhere] * 4 + [scalars] * 3,
+        out_specs=pl.BlockSpec(memory_space=pltpu.VMEM),
+        scratch_shapes=[
+            pltpu.VMEM((tp, CHUNKS, rows_each, kc), jnp.bfloat16),
+            pltpu.VMEM((CHUNKS, kc, width), jnp.bfloat16),
+            pltpu.VMEM((CHUNKS, slots_each, kc, rank), jnp.bfloat16),
+            pltpu.VMEM((nrows, owned, width), jnp.bfloat16),
+            pltpu.VMEM((tp, rows_each, width), jnp.float32),
+            pltpu.VMEM((tp, slots_each, rows_each, rank), jnp.float32),
+            pltpu.VMEM((tp, rows_each, width), jnp.bfloat16),
+            pltpu.VMEM((nrows, rows_each, width), jnp.bfloat16),
+            pltpu.VMEM((tp, rows_each, rank), jnp.float32),
+            pltpu.VMEM((nrows, rows_each, rank), jnp.float32),
+            pltpu.VMEM((rows_each, rank), jnp.float32),
+            pltpu.VMEM((tp, rows_each, rank), jnp.float32),
+            dma((CHUNKS,)), dma((CHUNKS,)), dma((CHUNKS,)), dma,
+            dma((nrows - 1,)), dma((nrows - 1,)),
+            dma((tp - 1, CHUNKS)), dma((tp - 1, CHUNKS)),
+            dma((tp - 1, CHUNKS)), dma((tp - 1, CHUNKS)),
+            dma((tp,)), dma((nrows,)), dma((tp,)), dma((nrows,)),
+            dma((tp - 1,)), dma((tp - 1,)),
+        ],
+        compiler_params=pltpu.CompilerParams(
+            collective_id=0, has_side_effects=True, vmem_limit_bytes=56 * 2**20
+        ),
+        cost_estimate=pl.CostEstimate(
+            flops=2 * tp * rows_each * depth * width,
+            bytes_accessed=2 * depth * width,
+            transcendentals=0,
+        ),
+    )(hidden, down_weight, first, second, seg_len, seg_ad, slot_of)
+
+
 def solution(mesh):
     placed = (
         P(("groups", "tp"), "rows"),
@@ -75,6 +381,8 @@
         P("groups", None),
         P(),
     )
+    tp, nrows = mesh.shape["tp"], mesh.shape["rows"]
+    body = functools.partial(fused, tp, nrows) if tp == nrows and tp <= 4 else local
     return jax.shard_map(
-        local, mesh=mesh, in_specs=placed, out_specs=P(("groups", "rows"), "tp"), check_vma=False
-    )
+        body, mesh=mesh, in_specs=placed, out_specs=P(("groups", "rows"), "tp"), check_vma=False
+    )

time: 231 us -> 88.9 us (0.38)
  waiting for transfers between devices: 191 us -> 0 us
  Pallas kernels: 0 us -> 82.4 us
  matrix products: 20.2 us -> 0 us
  between operations: 13.2 us -> 0.01 us
  other arithmetic: 4.94 us -> 0 us
  local copies, waits for them, and re-layouts: 1.66 us -> 6.23 us
    psum x1 -> x0, waiting for transfers between devices: 83.2 us -> none  [reduce_shrink(): return lax.psum(partial_low, ('tp', 'rows'))]
    pallas_call x0 -> x1, Pallas kernels: none -> 82.4 us  [fused(): pl.pallas_call(fused_kernel, out_shape=jax.ShapeDtypeStruct((rows_each, w...]
    all_gather x1 -> x0, waiting for transfers between devices: 73.8 us -> none  [local(): segment_piece = lax.all_gather(hidden, 'tp', axis=0, tiled=True)]
    reduce_scatter x1 -> x0, waiting for transfers between devices: 33.2 us -> none  [local(): lax.psum_scatter(part + low_rank, 'rows', scatter_dimension=0, tiled=True)]
    dot_general x3 -> x0, matrix products: 16.8 us -> none  [the longest x1 14.9 us: local(): jnp.dot(segment_piece, down_weight, preferred_element_type=jnp.float32)]
    unnamed x8 -> x2, local copies, waits for them, and re-layouts: 1.58 us -> 6.23 us
    unnamed x1 -> x0, matrix products: 3.44 us -> none
  transfers between devices with their start and end apart: 3 -> 0, of which waited for: 3 -> 0; matrix products, arithmetic and copies ran while one was open for 1% -> 0% of each run, Pallas kernels for 0% -> 0%
where the time goes in v1:
time: 88.9 us; the launch traced here: 88.7 us
  Pallas kernels  82.4 us (93%)
  local copies, waits for them, and re-layouts  6.23 us (7%)
    pallas_call x1, Pallas kernels, fused(): pl.pallas_call(fused_kernel, out_shape=jax.ShapeDtypeStruct((rows_each, w...  82.4 us
    unnamed x2, local copies, waits for them, and re-layouts  6.23 us

profile of v1, /device:TPU:0, one launch (start us, length us, event | category | flops | bytes accessed | tf_op | source)
XLA Modules:
  0.0 88.7 jit_solution(13373614400575411516)
XLA Ops:
  0.0 4.6 %copy.8.a = bf16[2,7168,64]{2,1,0:T(8,128)(2,1)} copy(bf16[2,7168,64]{1,2,0:T(8,128)(2,1)} %param.9) | data formatting | bytes 3670016 | tf_op args[2]
  4.6 82.4 %shard_map.73 = bf16[64,2048]{1,0:T(8,128)(2,1)} custom-call(bf16[64,7168]{1,0:T(8,128)(2,1)} %hid.1, bf16[7168,2048]{1,0:T(8,128)(2,1)} %w.1, bf16[2,7168,64]{2,1,0:T(8,128)(2,1)} %copy.8.a, bf16[128,2048]{1,0:T(8,128)(2,1)} %bitcast.1, s32[4,4]{1,0:T(4,128)} %seg_len.1, s32[4,4]{1,0:T(4,128)} %seg_ad.1, s32[8]{0:T(128)} %slot_of.1), custom_call_target="tpu_custom_call" | custom-call | flops 7516192768 | bytes 29360128 | tf_op jit(solution)/shard_map/pallas_call | solution.py:338
  87.0 1.7 %copy.10 = bf16[64,2048]{1,0:T(8,128)(2,1)} copy(bf16[64,2048]{1,0:T(8,128)(2,1)} %shard_map.73) | data formatting | bytes 524288

commit v2 on v1

--- a/solution.py
+++ b/solution.py
@@ -85,7 +85,7 @@
     tp, chunks, rows_each, kc = gath.shape
     nrows = rbuf.shape[0]
     slots_each = av.shape[1]
-    rank = av.shape[3]
+    rank = av.shape[2]
     width = wv.shape[2]
     tiles = width // TILE
     up, down = lax.rem(t + 1, tp), lax.rem(t + tp - 1, tp)
@@ -102,7 +102,7 @@
 
     def a_copy(c):
         return pltpu.make_async_copy(
-            a.at[:, pl.ds(pl.multiple_of(c * kc, kc), kc), :], av.at[c], a_sem.at[c]
+            a.at[:, :, pl.ds(pl.multiple_of(c * kc, kc), kc)], av.at[c], a_sem.at[c]
         )
 
     def b_own():
@@ -128,10 +128,10 @@
             device_id={"tp": down}, device_id_type=MESH,
         )
 
-    def base_copy(j, slot, sem):
-        return pltpu.make_async_remote_copy(
-            src_ref=stage.at[j], dst_ref=rbuf.at[slot],
-            send_sem=base_send.at[j], recv_sem=base_recv.at[sem],
+    def base_copy(j, n, slot):
+        return pltpu.make_async_remote_copy(
+            src_ref=stage.at[j, n], dst_ref=rbuf.at[slot, n],
+            send_sem=base_send.at[j, n], recv_sem=base_recv.at[slot, n],
             device_id={"rows": j}, device_id_type=MESH,
         )
 
@@ -151,35 +151,35 @@
 
     for c in range(chunks):
         own_copy(c).start()
+
+    barrier = pltpu.get_barrier_semaphore()
+    for d in range(1, tp):
+        pl.semaphore_signal(
+            barrier, inc=1, device_id={"tp": lax.rem(t + d, tp)}, device_id_type=MESH
+        )
+    for d in range(1, nrows):
+        pl.semaphore_signal(
+            barrier, inc=1, device_id={"rows": lax.rem(r + d, nrows)}, device_id_type=MESH
+        )
+    acc[...] = jnp.zeros_like(acc)
+    sh[...] = jnp.zeros_like(sh)
+    pl.semaphore_wait(barrier, tp - 1 + nrows - 1)
+
+    for c in range(chunks):
+        own_copy(c).wait()
+
+        @pl.when(t < tp - 1)
+        def _():
+            right(0, t, c).start()
+
+        @pl.when(t > 0)
+        def _():
+            left(0, t, c).start()
+
     for c in range(chunks):
         w_copy(c).start()
         a_copy(c).start()
     b_own().start()
-
-    barrier = pltpu.get_barrier_semaphore()
-    for d in range(1, tp):
-        pl.semaphore_signal(
-            barrier, inc=1, device_id={"tp": lax.rem(t + d, tp)}, device_id_type=MESH
-        )
-    for d in range(1, nrows):
-        pl.semaphore_signal(
-            barrier, inc=1, device_id={"rows": lax.rem(r + d, nrows)}, device_id_type=MESH
-        )
-    acc[...] = jnp.zeros_like(acc)
-    sh[...] = jnp.zeros_like(sh)
-    pl.semaphore_wait(barrier, tp - 1 + nrows - 1)
-
-    for c in range(chunks):
-        own_copy(c).wait()
-
-        @pl.when(t < tp - 1)
-        def _():
-            right(0, t, c).start()
-
-        @pl.when(t > 0)
-        def _():
-            left(0, t, c).start()
-
     for d in range(1, nrows):
         b_copy(d).start()
 
@@ -193,32 +193,44 @@
         return slot
 
     def compute(shard, c):
-        for q in range(slots_each):
-            sh[shard, q] += jnp.dot(
-                gath[shard, c], av[c, q], preferred_element_type=jnp.float32
-            )
+        last = c == chunks - 1
+        piece = gath[shard, c]
+        sh[shard] += lax.dot_general(
+            piece, av[c].reshape(slots_each * rank, kc), (((1,), (1,)), ((), ())),
+            preferred_element_type=jnp.float32,
+        )
+
+        @pl.when(last)
+        def _():
+            send_shrink(shard)
 
         def tile_step(n, carry):
             cols = pl.ds(pl.multiple_of(n * TILE, TILE), TILE)
-            acc[shard, :, cols] += jnp.dot(
+            acc[shard, n] += jnp.dot(
                 gath[shard, c], wv[c, :, cols], preferred_element_type=jnp.float32
             )
+
+            @pl.when(last & (shard != r))
+            def _():
+                stage[shard, n] = acc[shard, n].astype(jnp.bfloat16)
+                base_copy(shard, n, r).start()
+
             return carry
 
         lax.fori_loop(0, tiles, tile_step, 0)
 
-    def finish(j):
+    def send_shrink(j):
         slot = slots_in(j)
         picked = jnp.zeros((rows_each, rank), jnp.float32)
         for q in range(slots_each):
-            picked += jnp.where(slot == t * slots_each + q, sh[j, q], 0.0)
+            picked += jnp.where(
+                slot == t * slots_each + q, sh[j, :, q * rank:(q + 1) * rank], 0.0
+            )
         shsel[j] = picked
 
         @pl.when(j != r)
         def _():
             sh_copy(j, r, r).start()
-            stage[j] = acc[j].astype(jnp.bfloat16)
-            base_copy(j, r, r).start()
 
     def own_step(c, carry):
         w_copy(c).wait()
@@ -227,7 +239,6 @@
         return carry
 
     lax.fori_loop(0, chunks, own_step, 0)
-    finish(t)
 
     def ring_step(i, carry):
         s, c = i // chunks, i % chunks
@@ -243,10 +254,6 @@
 
             compute(low, c)
 
-            @pl.when(c == chunks - 1)
-            def _():
-                finish(low)
-
         @pl.when(high <= tp - 1)
         def _():
             left(s, high, c).wait_recv()
@@ -256,10 +263,6 @@
                 left(s + 1, high, c).start()
 
             compute(high, c)
-
-            @pl.when(c == chunks - 1)
-            def _():
-                finish(high)
 
         return carry
 
@@ -287,20 +290,20 @@
     upper = spread.astype(jnp.bfloat16)
     lower = (spread - upper.astype(jnp.float32)).astype(jnp.bfloat16)
     pair = jnp.concatenate([upper, lower], axis=0)
-    for d in range(1, nrows):
-        other = lax.rem(r + d, nrows)
-        base_copy(other, other, other).wait_recv()
     depth = bv.shape[0] * bv.shape[1]
     for n in range(tiles):
-        cols = slice(n * TILE, (n + 1) * TILE)
         both = jnp.dot(
-            pair, bv[:, :, cols].reshape(depth, TILE), preferred_element_type=jnp.float32
-        )
-        value = both[:rows_each] + both[rows_each:] + acc[r, :, cols]
+            pair, bv[:, :, n * TILE:(n + 1) * TILE].reshape(depth, TILE),
+            preferred_element_type=jnp.float32,
+        )
+        acc[r, n] += both[:rows_each] + both[rows_each:]
+    for n in range(tiles):
+        value = acc[r, n]
         for d in range(1, nrows):
             other = lax.rem(r + d, nrows)
-            value += rbuf[other, :, cols].astype(jnp.float32)
-        out[:, cols] = value.astype(out.dtype)
+            base_copy(other, n, other).wait_recv()
+            value += rbuf[other, n].astype(jnp.float32)
+        out[:, n * TILE:(n + 1) * TILE] = value.astype(out.dtype)
 
     def drain(i, carry):
         s, c = i // chunks, i % chunks
@@ -320,7 +323,8 @@
         other = lax.rem(r + d, nrows)
         b_copy(d).wait_send()
         sh_copy(other, r, r).wait_send()
-        base_copy(other, r, r).wait_send()
+        for n in range(tiles):
+            base_copy(other, n, r).wait_send()
     for d in range(1, tp):
         z_copy(d, t).wait_send()
 
@@ -330,6 +334,7 @@
     width = down_weight.shape[1]
     kc = depth // CHUNKS
     slots_each, _, rank = first.shape
+    first = first.transpose(0, 2, 1)
     owned = second.shape[0] * second.shape[1]
     second = second.reshape(owned, width)
     dma = pltpu.SemaphoreType.DMA
@@ -343,12 +348,12 @@
         scratch_shapes=[
             pltpu.VMEM((tp, CHUNKS, rows_each, kc), jnp.bfloat16),
             pltpu.VMEM((CHUNKS, kc, width), jnp.bfloat16),
-            pltpu.VMEM((CHUNKS, slots_each, kc, rank), jnp.bfloat16),
+            pltpu.VMEM((CHUNKS, slots_each, rank, kc), jnp.bfloat16),
             pltpu.VMEM((nrows, owned, width), jnp.bfloat16),
-            pltpu.VMEM((tp, rows_each, width), jnp.float32),
-            pltpu.VMEM((tp, slots_each, rows_each, rank), jnp.float32),
-            pltpu.VMEM((tp, rows_each, width), jnp.bfloat16),
-            pltpu.VMEM((nrows, rows_each, width), jnp.bfloat16),
+            pltpu.VMEM((tp, width // TILE, rows_each, TILE), jnp.float32),
+            pltpu.VMEM((tp, rows_each, slots_each * rank), jnp.float32),
+            pltpu.VMEM((tp, width // TILE, rows_each, TILE), jnp.bfloat16),
+            pltpu.VMEM((nrows, width // TILE, rows_each, TILE), jnp.bfloat16),
             pltpu.VMEM((tp, rows_each, rank), jnp.float32),
             pltpu.VMEM((nrows, rows_each, rank), jnp.float32),
             pltpu.VMEM((rows_each, rank), jnp.float32),
@@ -357,7 +362,7 @@
             dma((nrows - 1,)), dma((nrows - 1,)),
             dma((tp - 1, CHUNKS)), dma((tp - 1, CHUNKS)),
             dma((tp - 1, CHUNKS)), dma((tp - 1, CHUNKS)),
-            dma((tp,)), dma((nrows,)), dma((tp,)), dma((nrows,)),
+            dma((tp, width // TILE)), dma((nrows, width // TILE)), dma((tp,)), dma((nrows,)),
             dma((tp - 1,)), dma((tp - 1,)),
         ],
         compiler_params=pltpu.CompilerParams(

time: 88.9 us -> 78.8 us (0.89)
  Pallas kernels: 82.4 us -> 76.9 us
  local copies, waits for them, and re-layouts: 6.23 us -> 1.67 us
    pallas_call x1, Pallas kernels: 82.4 us -> 76.9 us  [fused(): pl.pallas_call(fused_kernel, out_shape=jax.ShapeDtypeStruct((rows_each, w...]
    unnamed x2 -> x1, local copies, waits for them, and re-layouts: 6.23 us -> 1.67 us
where the time goes in v2:
time: 78.8 us; the launch traced here: 78.6 us
  Pallas kernels  76.9 us (98%)
  local copies, waits for them, and re-layouts  1.67 us (2%)
    pallas_call x1, Pallas kernels, fused(): pl.pallas_call(fused_kernel, out_shape=jax.ShapeDtypeStruct((rows_each, w...  76.9 us
    unnamed x1, local copies, waits for them, and re-layouts  1.67 us

profile of v2, /device:TPU:0, one launch (start us, length us, event | category | flops | bytes accessed | tf_op | source)
XLA Modules:
  0.0 78.6 jit_solution(10471750611739060422)
XLA Ops:
  0.0 76.9 %shard_map.73 = bf16[64,2048]{1,0:T(8,128)(2,1)} custom-call(bf16[64,7168]{1,0:T(8,128)(2,1)} %hid.1, bf16[7168,2048]{1,0:T(8,128)(2,1)} %w.1, bf16[2,64,7168]{2,1,0:T(8,128)(2,1)} %bitcast.2, bf16[128,2048]{1,0:T(8,128)(2,1)} %bitcast.3, s32[4,4]{1,0:T(4,128)} %seg_len.1, s32[4,4]{1,0:T(4,128)} %seg_ad.1, s32[8]{0:T(128)} %slot_of.1), custom_call_target="tpu_custom_call" | custom-call | flops 7516192768 | bytes 29360128 | tf_op jit(solution)/shard_map/pallas_call | solution.py:343
  77.0 1.7 %copy.9 = bf16[64,2048]{1,0:T(8,128)(2,1)} copy(bf16[64,2048]{1,0:T(8,128)(2,1)} %shard_map.73) | data formatting | bytes 524288

commit v3 on v2

--- a/solution.py
+++ b/solution.py
@@ -76,18 +76,22 @@
 
 def fused_kernel(
     hid, w, a, b, seg_len, seg_ad, slot_of, out,
-    gath, wv, av, bv, acc, sh, stage, rbuf, shsel, shbuf, zsrc, zbuf,
+    gath, wv, av, bv, acc, sh, stage, rbuf, mbuf, shsel, shbuf, zsrc, zbuf,
     own_sem, w_sem, a_sem, bown_sem, b_send, b_recv,
     right_send, right_recv, left_send, left_recv,
-    base_send, base_recv, sh_send, sh_recv, z_send, z_recv,
+    base_send, base_recv, mate_send, mate_recv, sh_send, sh_recv, z_send, z_recv,
 ):
     t, r = lax.axis_index("tp"), lax.axis_index("rows")
     tp, chunks, rows_each, kc = gath.shape
-    nrows = rbuf.shape[0]
+    nrows = shbuf.shape[0]
     slots_each = av.shape[1]
     rank = av.shape[2]
     width = wv.shape[2]
     tiles = width // TILE
+    part = tiles // 2
+    core, chip = r % 2, r // 2
+    mate = r + 1 - 2 * core
+    late = ((t == 0) & (r == tp - 1)) | ((t == tp - 1) & (r == 0))
     up, down = lax.rem(t + 1, tp), lax.rem(t + tp - 1, tp)
 
     def own_copy(c):
@@ -133,6 +137,13 @@
             src_ref=stage.at[j, n], dst_ref=rbuf.at[slot, n],
             send_sem=base_send.at[j, n], recv_sem=base_recv.at[slot, n],
             device_id={"rows": j}, device_id_type=MESH,
+        )
+
+    def mate_copy(j, n):
+        return pltpu.make_async_remote_copy(
+            src_ref=stage.at[j, n], dst_ref=mbuf.at[j, n],
+            send_sem=mate_send.at[j, n], recv_sem=mate_recv.at[j, n],
+            device_id={"rows": mate}, device_id_type=MESH,
         )
 
     def sh_copy(j, slot, sem):
@@ -192,6 +203,16 @@
             end = end + seg_len[j, k]
         return slot
 
+    def exchange_shrink():
+        total = shsel[r]
+        for d in range(1, nrows):
+            other = lax.rem(r + d, nrows)
+            sh_copy(other, other, other).wait_recv()
+            total = total + shbuf[other]
+        zsrc[...] = total
+        for d in range(1, tp):
+            z_copy(d, t).start()
+
     def compute(shard, c):
         last = c == chunks - 1
         piece = gath[shard, c]
@@ -204,16 +225,33 @@
         def _():
             send_shrink(shard)
 
-        def tile_step(n, carry):
+        def tile_step(m, carry):
+            n = lax.rem(m + (1 - core) * part, tiles)
             cols = pl.ds(pl.multiple_of(n * TILE, TILE), TILE)
+            @pl.when(last & (shard == r) & late & (m == 1))
+            def _():
+                exchange_shrink()
+
             acc[shard, n] += jnp.dot(
                 gath[shard, c], wv[c, :, cols], preferred_element_type=jnp.float32
             )
 
-            @pl.when(last & (shard != r))
+            @pl.when(last & (shard == mate))
             def _():
                 stage[shard, n] = acc[shard, n].astype(jnp.bfloat16)
-                base_copy(shard, n, r).start()
+                base_copy(shard, n, 0).start()
+
+            @pl.when(last & (shard // 2 != chip) & (m < part))
+            def _():
+                stage[shard, n] = acc[shard, n].astype(jnp.bfloat16)
+                mate_copy(shard, n).start()
+
+            @pl.when(last & (shard // 2 != chip) & (m >= part))
+            def _():
+                mate_copy(shard, n).wait_recv()
+                both = acc[shard, n] + mbuf[shard, n].astype(jnp.float32)
+                stage[shard, n] = both.astype(jnp.bfloat16)
+                base_copy(shard, n, 1).start()
 
             return carry
 
@@ -244,6 +282,10 @@
         s, c = i // chunks, i % chunks
         low, high = t - 1 - s, t + 1 + s
 
+        @pl.when((i == (tp - 1) * chunks - 1) & jnp.logical_not(late))
+        def _():
+            exchange_shrink()
+
         @pl.when(low >= 0)
         def _():
             right(s, low, c).wait_recv()
@@ -268,14 +310,7 @@
 
     lax.fori_loop(0, (tp - 1) * chunks, ring_step, 0)
 
-    total = shsel[r]
-    for d in range(1, nrows):
-        other = lax.rem(r + d, nrows)
-        sh_copy(other, other, other).wait_recv()
-        total = total + shbuf[other]
-    zsrc[...] = total
-    for d in range(1, tp):
-        z_copy(d, t).start()
+    total = zsrc[...]
     b_own().wait()
     for d in range(1, nrows):
         b_copy(d).wait_recv()
@@ -299,10 +334,9 @@
         acc[r, n] += both[:rows_each] + both[rows_each:]
     for n in range(tiles):
         value = acc[r, n]
-        for d in range(1, nrows):
-            other = lax.rem(r + d, nrows)
-            base_copy(other, n, other).wait_recv()
-            value += rbuf[other, n].astype(jnp.float32)
+        for k in range(2):
+            base_copy(mate, n, k).wait_recv()
+            value += rbuf[k, n].astype(jnp.float32)
         out[:, n * TILE:(n + 1) * TILE] = value.astype(out.dtype)
 
     def drain(i, carry):
@@ -323,8 +357,13 @@
         other = lax.rem(r + d, nrows)
         b_copy(d).wait_send()
         sh_copy(other, r, r).wait_send()
-        for n in range(tiles):
-            base_copy(other, n, r).wait_send()
+    for n in range(tiles):
+        base_copy(mate, n, 0).wait_send()
+    for k in range(2):
+        far = 2 * (1 - chip) + k
+        for m in range(part):
+            mate_copy(far, (1 - core) * part + m).wait_send()
+            base_copy(far, core * part + m, 1).wait_send()
     for d in range(1, tp):
         z_copy(d, t).wait_send()
 
@@ -353,7 +392,8 @@
             pltpu.VMEM((tp, width // TILE, rows_each, TILE), jnp.float32),
             pltpu.VMEM((tp, rows_each, slots_each * rank), jnp.float32),
             pltpu.VMEM((tp, width // TILE, rows_each, TILE), jnp.bfloat16),
-            pltpu.VMEM((nrows, width // TILE, rows_each, TILE), jnp.bfloat16),
+            pltpu.VMEM((2, width // TILE, rows_each, TILE), jnp.bfloat16),
+            pltpu.VMEM((tp, width // TILE, rows_each, TILE), jnp.bfloat16),
             pltpu.VMEM((tp, rows_each, rank), jnp.float32),
             pltpu.VMEM((nrows, rows_each, rank), jnp.float32),
             pltpu.VMEM((rows_each, rank), jnp.float32),
@@ -362,7 +402,8 @@
             dma((nrows - 1,)), dma((nrows - 1,)),
             dma((tp - 1, CHUNKS)), dma((tp - 1, CHUNKS)),
             dma((tp - 1, CHUNKS)), dma((tp - 1, CHUNKS)),
-            dma((tp, width // TILE)), dma((nrows, width // TILE)), dma((tp,)), dma((nrows,)),
+            dma((tp, width // TILE)), dma((2, width // TILE)),
+            dma((tp, width // TILE)), dma((tp, width // TILE)), dma((tp,)), dma((nrows,)),
             dma((tp - 1,)), dma((tp - 1,)),
         ],
         compiler_params=pltpu.CompilerParams(
@@ -387,7 +428,7 @@
         P(),
     )
     tp, nrows = mesh.shape["tp"], mesh.shape["rows"]
-    body = functools.partial(fused, tp, nrows) if tp == nrows and tp <= 4 else local
+    body = functools.partial(fused, tp, nrows) if tp == nrows == 4 else local
     return jax.shard_map(
         body, mesh=mesh, in_specs=placed, out_specs=P(("groups", "rows"), "tp"), check_vma=False
     )

time: 78.8 us -> 78.6 us (level)
  no operation moved by 1% of the time
where the time goes in v3:
time: 78.6 us; the launch traced here: 78.4 us
  Pallas kernels  76.7 us (98%)
  local copies, waits for them, and re-layouts  1.67 us (2%)
    pallas_call x1, Pallas kernels, fused(): pl.pallas_call(fused_kernel, out_shape=jax.ShapeDtypeStruct((rows_each, w...  76.7 us
    unnamed x1, local copies, waits for them, and re-layouts  1.67 us

profile of v3, /device:TPU:0, one launch (start us, length us, event | category | flops | bytes accessed | tf_op | source)
XLA Modules:
  0.0 78.4 jit_solution(9377543713145464727)
XLA Ops:
  0.0 76.7 %shard_map.73 = bf16[64,2048]{1,0:T(8,128)(2,1)} custom-call(bf16[64,7168]{1,0:T(8,128)(2,1)} %hid.1, bf16[7168,2048]{1,0:T(8,128)(2,1)} %w.1, bf16[2,64,7168]{2,1,0:T(8,128)(2,1)} %bitcast.2, bf16[128,2048]{1,0:T(8,128)(2,1)} %bitcast.3, s32[4,4]{1,0:T(4,128)} %seg_len.1, s32[4,4]{1,0:T(4,128)} %seg_ad.1, s32[8]{0:T(128)} %slot_of.1), custom_call_target="tpu_custom_call" | custom-call | flops 7516192768 | bytes 29360128 | tf_op jit(solution)/shard_map/pallas_call | solution.py:382
  76.7 1.7 %copy.9 = bf16[64,2048]{1,0:T(8,128)(2,1)} copy(bf16[64,2048]{1,0:T(8,128)(2,1)} %shard_map.73) | data formatting | bytes 524288
